TPU v7x, 32 devices: a whole 2x2x4 slice. The times are simulated.
32 devices in a mesh: inner: 16 (over z, y, x), outer: 2 (over core).
Axes of the slice: x: 2, y: 2, z: 4, core: 2. Of those that a mesh axis runs over, the one named last changes fastest.
Arguments:
- feats_first: bfloat16 [2, 4096, 2048], P('outer', 'inner'), may hold values from -4 to 8
- feats_second: bfloat16 [2, 4096, 2048], P('outer', 'inner'), may hold values from -4 to 8
- expander: bfloat16 [2048, 1024], P('inner'), may hold values from -0.125 to 0.125
- tile_count: int32 [2, 16], replicated, may hold values from 64 to 256, as said below
- match_dev: int32 [2, 4096, 1], P('outer', 'inner'), may hold values from 0 to 15; in each aligned block of 256 rows (0 to 255, 256 to 511, ..., all dimensions but the last counted through in order) at most 48 rows name the same one
- match_tile: int32 [2, 4096], P('outer', 'inner'), may hold values from 0 to 255
Outputs:
- covariance: float32 [1024, 1024], P('inner')
- invariance: float32 [2, 4096], P('outer', 'inner')
Inputs may be any that keep to these rules, and one draw needn't show every extreme that they name: `tile_count`: for every slide some device has all 256 tiles live; the others at least a quarter. `match_dev`: at most 48 tiles of one device name the same device.
All inputs are finite; a program needn't handle non-finite values.
Results may differ from a plain program's by a relative error of at most 0.00135.
Values may be sent and summed in bfloat16 or wider, within the bound.
A program may use at most 64 MiB of HBM per device.

v0:
```python
import jax
import jax.numpy as jnp
from jax import lax
from jax.sharding import PartitionSpec as P


def shards(feats_first, feats_second, expander, tile_count, match_dev, match_tile):
    first_rows = feats_first[0]
    second_rows = feats_second[0]
    tile_rows = first_rows.shape[0]
    expand_width = expander.shape[1]
    group_size = lax.axis_size("inner")
    capacity = max(2, 3 * tile_rows // group_size)
    inner_pos = lax.axis_index("inner")
    outer_pos = lax.axis_index("outer")
    piece = lax.all_gather(expander, "inner", axis=0, tiled=True)
    first_acc = jnp.dot(first_rows, piece, preferred_element_type=jnp.float32)
    second_acc = jnp.dot(second_rows, piece, preferred_element_type=jnp.float32)
    first_embed = first_acc.astype(jnp.bfloat16)
    second_embed = second_acc.astype(jnp.bfloat16)
    counts = lax.dynamic_index_in_dim(tile_count, outer_pos, 0, keepdims=False)
    own_count = lax.dynamic_index_in_dim(counts, inner_pos, 0, keepdims=False)
    row_index = jnp.arange(tile_rows, dtype=jnp.int32)
    live = row_index < own_count
    target_dev = match_dev[0, :, 0]
    target_tile = match_tile[0]
    onehot = (target_dev[:, None] == jnp.arange(group_size, dtype=jnp.int32)[None, :]).astype(
        jnp.int32
    )
    slot_pos = jnp.sum((jnp.cumsum(onehot, axis=0) - 1) * onehot, axis=1)
    send_rows = (
        jnp.zeros((group_size, capacity, expand_width), jnp.bfloat16)
        .at[target_dev, slot_pos]
        .set(first_embed)
    )
    send_tiles = (
        jnp.zeros((group_size, capacity), jnp.int32).at[target_dev, slot_pos].set(target_tile)
    )
    recv_rows, recv_tiles = (
        lax.all_to_all(send_rows, "inner", split_axis=0, concat_axis=0, tiled=True),
        lax.all_to_all(send_tiles, "inner", split_axis=0, concat_axis=0, tiled=True),
    )
    partner = second_embed[recv_tiles]
    diff = recv_rows.astype(jnp.float32) - partner.astype(jnp.float32)
    distance = jnp.where(recv_tiles < own_count, jnp.mean(diff * diff, axis=-1), jnp.float32(0.0))
    returned = lax.all_to_all(distance, "inner", split_axis=0, concat_axis=0, tiled=True)
    dest_count = counts[target_dev]
    valid = live & (target_tile < dest_count)
    invariance = jnp.where(valid, returned[target_dev, slot_pos], jnp.float32(0.0))
    masked = jnp.where(live[:, None], first_embed, jnp.zeros_like(first_embed))
    column_total = lax.psum(jnp.sum(masked.astype(jnp.float32), axis=0), ("inner", "outer"))
    total = jnp.sum(tile_count).astype(jnp.float32)
    share_rows = expand_width // group_size
    local_share = lax.psum_scatter(
        lax.dot_general(
            masked, masked, (((0,), (0,)), ((), ())), preferred_element_type=jnp.float32
        ),
        "inner",
        scatter_dimension=0,
        tiled=True,
    )
    gram_share = lax.psum(local_share, "outer")
    own_sums = lax.dynamic_slice_in_dim(column_total, inner_pos * share_rows, share_rows, 0)
    covariance = (gram_share - own_sums[:, None] * column_total[None, :] / total) / (total - 1.0)
    return (covariance, invariance[None, :])


def solution(mesh):
    return jax.shard_map(
        shards,
        mesh=mesh,
        in_specs=(
            P("outer", "inner", None),
            P("outer", "inner", None),
            P("inner", None),
            P(),
            P("outer", "inner", None),
            P("outer", "inner"),
        ),
        out_specs=(P("inner", None), P("outer", "inner")),
        check_vma=False,
    )
```

profile of v0, /device:TPU:0, one launch (start us, length us, event | category | flops | bytes accessed | tf_op | source)
XLA Modules:
  0.0 292.9 jit_solution(2286077928159644080)
XLA Ops:
  7.2 0.7 all-gather.2.cloned.1.call-update
  8.0 1.3 dynamic_slice.11
  9.3 0.6 iota_compare_fusion.2
  10.0 79.6 %all-gather.2.cloned.1.call-done = bf16[2048,1024]{1,0:T(8,128)(2,1)} async-done(((bf16[128,1024]{1,0:T(8,128)(2,1)}), bf16[2048,1024]{1,0:T(8,128)(2,1)}) %all-gather.2.cloned.1.call-update) | async-done | bytes 4194320 | tf_op jit(solution)/shard_map/all_gather | solution.py:16
  89.6 3.4 %convert_reduce_fusion = (f32[1024]{0:T(1024)S(1)}, bf16[256,1024]{1,0:T(8,128)(2,1)S(1)}) fusion(pred[256]{0:T(512)(128)(4,1)S(1)} %iota_compare_fusion.2, bf16[2048,1024]{1,0:T(8,128)(2,1)} %all-gather.2.cloned.1.call-done, bf16[1,256,2048]{2,1,0:T(8,128)(2,1)S(1)} %copy-done), kind=kOutput, calls=%fused_computation.11 | convolution fusion | flops 1074789376 | bytes 5771520 | tf_op jit(solution)/shard_map/dot_general | solution.py:17
  93.1 2.8 fusion.4
  95.9 0.6 copy-done.1
  96.5 0.6 reduce-window.6
  97.1 0.2 slice_reduce_fusion
  97.3 0.7 fusion.11
  98.1 0.1 fusion.6
  98.1 4.3 %compare_select_fusion.4 = (s32[256,1]{0,1:T(1,128)S(1)}, s32[256,1]{0,1:T(1,128)S(1)}) fusion(s32[]{:T(128)} %bitcast.12, s32[]{:T(128)} %bitcast.13, s32[]{:T(128)} %bitcast.14, s32[]{:T(128)} %bitcast.15, s32[]{:T(128)} %bitcast.16, s32[]{:T(128)} %bitcast.18, s32[]{:T(128)} %bitcast.17, s32[1,256,1]{1,2,0:T(1,128)S(1)} %copy-done.1), kind=kLoop, calls=%fused_computation.38 | loop fusion | flops 3840 | bytes 3100 | tf_op jit(solution)/shard_map/gather | solution.py:47
  102.4 0.6 broadcast.105
  103.0 36.1 %scatter_fusion = s32[16,48]{1,0:T(8,128)} fusion(s32[16,48]{1,0:T(8,128)} %broadcast.105, s32[256]{0:T(256)S(1)} %bitcast.67, s32[256]{0:T(256)S(1)} %bitcast.75), kind=kCustom, calls=%fused_computation.2 | custom fusion | bytes 5120 | tf_op jit(solution)/shard_map/scatter | solution.py:37
  139.2 4.4 %all-to-all-start = ((s32[16,1,48]{2,1,0:T(1,128)}), s32[16,1,48]{2,1,0:T(1,128)S(1)}, u32[]{:S(2)}, u32[]{:S(2)}) async-start(s32[16,1,48]{2,1,0:T(1,128)} %bitcast.28), calls=%async_computation.1 | async-start | bytes 16384 | tf_op jit(solution)/shard_map/all_to_all | solution.py:41
  143.6 1.4 broadcast_in_dim.22
  145.0 36.8 %scatter_fusion.1 = bf16[16,48,1024]{2,1,0:T(8,128)(2,1)} fusion(bf16[16,48,1024]{2,1,0:T(8,128)(2,1)} %broadcast_in_dim.22, s32[256]{0:T(256)S(1)} %bitcast.68, bf16[256,1024]{1,0:T(8,128)(2,1)S(1)} %get-tuple-element.32), kind=kCustom, calls=%fused_computation.3 | custom fusion | bytes 1574912 | tf_op jit(solution)/shard_map/scatter | solution.py:34
  181.8 7.1 %all-to-all-start.1 = ((bf16[16,48,1024]{2,1,0:T(8,128)(2,1)}), bf16[16,48,1024]{2,1,0:T(8,128)(2,1)S(1)}, u32[]{:S(2)}, u32[]{:S(2)}) async-start(bf16[16,48,1024]{2,1,0:T(8,128)(2,1)} %scatter_fusion.1), calls=%async_computation.2 | async-start | bytes 3145728 | tf_op jit(solution)/shard_map/all_to_all | solution.py:40
  189.0 0.1 reshape.148
  189.0 3.8 %convolution_convert_fusion = bf16[256,1024]{1,0:T(8,128)(2,1)S(1)} fusion(bf16[2048,1024]{1,0:T(8,128)(2,1)} %all-gather.2.cloned.1.call-done, bf16[1,256,2048]{2,1,0:T(8,128)(2,1)} %param.7), kind=kOutput, calls=%fused_computation.7 | convolution fusion | flops 1074003968 | bytes 5767168 | tf_op jit(solution)/shard_map/dot_general | solution.py:18
  192.8 3.6 %gather_fusion = bf16[768,1024]{1,0:T(8,128)(2,1)} fusion(bf16[256,1024]{1,0:T(8,128)(2,1)S(1)} %convolution_convert_fusion, s32[1024]{0:T(1024)S(1)} %pad_clamp_fusion), kind=kCustom, calls=%fused_computation | custom fusion | bytes 3148800 | tf_op jit(solution)/shard_map/gather | solution.py:43
  196.4 26.0 %all-to-all-done.1 = bf16[16,48,1024]{2,1,0:T(8,128)(2,1)S(1)} async-done(((bf16[16,48,1024]{2,1,0:T(8,128)(2,1)}), bf16[16,48,1024]{2,1,0:T(8,128)(2,1)S(1)}, u32[]{:S(2)}, u32[]{:S(2)}) %all-to-all-start.1) | async-done | bytes 1572896 | tf_op jit(solution)/shard_map/all_to_all | solution.py:40
  222.4 2.0 fusion.1
  224.4 1.2 compare_select_fusion
  225.6 7.3 %all-to-all-start.2 = ((f32[16,1,48]{2,1,0:T(1,128)}), f32[16,1,48]{2,1,0:T(1,128)S(1)}, u32[]{:S(2)}, u32[]{:S(2)}) async-start(f32[16,1,48]{2,1,0:T(1,128)} %compare_select_fusion), calls=%async_computation.3 | async-start | bytes 16384 | tf_op jit(solution)/shard_map/all_to_all | solution.py:46
  233.0 0.7 all-reduce.2.cloned.1.call-update
  233.7 5.6 %select_select_fusion = s32[256]{0:T(256)S(1)} fusion(pred[256]{0:T(512)(128)(4,1)S(1)} %get-tuple-element.10, pred[256]{0:T(512)(128)(4,1)S(1)} %get-tuple-element.9, pred[256]{0:T(512)(128)(4,1)S(1)} %get-tuple-element.8, pred[256]{0:T(512)(128)(4,1)S(1)} %get-tuple-element.7, pred[256]{0:T(512)(128)(4,1)S(1)} %get-tuple-element.6, ...), kind=kLoop, calls=%fused_computation.49 | loop fusion | flops 2304 | bytes 4388 | tf_op jit(solution)/shard_map/gather | solution.py:47
  239.3 0.6 reduce_sum.39
  240.6 40.7 %psum.15 = f32[1024]{0:T(1024)S(1)} all-reduce(f32[1024]{0:T(1024)S(1)} %get-tuple-element.31), channel_id=1, replica_groups=mesh['inner'=16,'outer'=2] {'inner','outer'}, use_global_device_ids=true, to_apply=%region_3.4 | all-reduce | flops 1024 | bytes 8192 | tf_op jit(solution)/shard_map/psum | solution.py:51
  281.4 1.9 gather_fusion.1
  283.4 1.2 and_select_fusion
  284.6 1.8 subtract_divide_fusion
  (25 shorter events, 0.4 us)
Async XLA Ops:
  7.2 82.4 %copy-start = (bf16[1,256,2048]{2,1,0:T(8,128)(2,1)S(1)}, bf16[1,256,2048]{2,1,0:T(8,128)(2,1)}, u32[]{:S(2)}) copy-start(bf16[1,256,2048]{2,1,0:T(8,128)(2,1)} %param.6) | copy-start | bytes 3145732
  7.2 82.4 %all-gather.2.cloned.1.call-start = ((), (), s32[]{:S(2)}) async-start(), calls=%async_computation.4 | async-start | bytes 4456448 | tf_op jit(solution)/shard_map/all_gather | solution.py:16
  7.9 225.1 %reduce-scatter.2.cloned.1.call-start = ((), (), s32[]{:S(2)}) async-start(), calls=%async_computation.5 | async-start | bytes 4456448 | tf_op jit(solution)/shard_map/reduce_scatter | solution.py:54
  95.8 0.7 copy-start.1
  95.8 1.5 copy-start.3
  95.8 7.2 %copy-start.2 = (s32[1,256]{1,0:T(1,128)S(1)}, s32[1,256]{1,0:T(1,128)}, u32[]{:S(2)}) copy-start(s32[1,256]{1,0:T(1,128)} %param.11) | copy-start | bytes 3076
  139.2 42.6 %all-to-all-start = ((s32[16,1,48]{2,1,0:T(1,128)}), s32[16,1,48]{2,1,0:T(1,128)S(1)}, u32[]{:S(2)}, u32[]{:S(2)}) async-start(s32[16,1,48]{2,1,0:T(1,128)} %bitcast.28), calls=%async_computation.1 | async-start | bytes 16384 | tf_op jit(solution)/shard_map/all_to_all | solution.py:41
  181.8 40.6 %all-to-all-start.1 = ((bf16[16,48,1024]{2,1,0:T(8,128)(2,1)}), bf16[16,48,1024]{2,1,0:T(8,128)(2,1)S(1)}, u32[]{:S(2)}, u32[]{:S(2)}) async-start(bf16[16,48,1024]{2,1,0:T(8,128)(2,1)} %scatter_fusion.1), calls=%async_computation.2 | async-start | bytes 3145728 | tf_op jit(solution)/shard_map/all_to_all | solution.py:40
  225.6 55.8 %all-to-all-start.2 = ((f32[16,1,48]{2,1,0:T(1,128)}), f32[16,1,48]{2,1,0:T(1,128)S(1)}, u32[]{:S(2)}, u32[]{:S(2)}) async-start(f32[16,1,48]{2,1,0:T(1,128)} %compare_select_fusion), calls=%async_computation.3 | async-start | bytes 16384 | tf_op jit(solution)/shard_map/all_to_all | solution.py:46
  233.0 51.6 %all-reduce.2.cloned.1.call-start = ((), (), s32[]{:S(2)}) async-start(), calls=%async_computation.6 | async-start | bytes 524288 | tf_op jit(solution)/shard_map/psum | solution.py:62
Sparse Core Ops, SparseCore 0:
  10.8 78.7 all-gather.1
  96.0 93.7 reduce-scatter.1
  236.1 19.5 all-reduce.1
where the time goes:
time: 296 us; the launch traced here: 293 us
  waiting for transfers between devices  107 us (36%)
  local copies, waits for them, and re-layouts  83.5 us (28%)
  blocking collectives  40.7 us (14%)
  starting transfers between devices  18.9 us (6%)
  other arithmetic  18.1 us (6%)
  between operations  14.5 us (5%)
  matrix products  10 us (3%)
    all_gather x1, waiting for transfers between devices, shards(): piece = lax.all_gather(expander, 'inner', axis=0, tiled=True)  79.6 us
    psum x1, blocking collectives, shards(): lax.psum(jnp.sum(masked.astype(jnp.float32), axis=0), ('inner', 'outer'))  40.7 us
    scatter x1, local copies, waits for them, and re-layouts, shards(): send_rows = jnp.zeros((group_size, capacity, expand_width), jnp.bfloat16)...  36.8 us
    scatter x1, local copies, waits for them, and re-layouts, shards(): jnp.zeros((group_size, capacity), jnp.int32).at[target_dev, slot_pos]  36.1 us
    all_to_all x1, waiting for transfers between devices, shards(): lax.all_to_all(send_rows, 'inner', split_axis=0, concat_axis=0, tiled=True)  26 us
    gather x3, other arithmetic, shards(): dest_count = counts[target_dev]  9.95 us
    all_to_all x1, starting transfers between devices, shards(): lax.all_to_all(distance, 'inner', split_axis=0, concat_axis=0, tiled=True)  7.3 us
    all_to_all x1, starting transfers between devices, shards(): lax.all_to_all(send_rows, 'inner', split_axis=0, concat_axis=0, tiled=True)  7.08 us
  transfers between devices with their start and end apart: 6, of which 2 were waited for; matrix products, arithmetic and copies ran while one was open for 35% of the time, Pallas kernels for 0%

commit v1 on v0

--- a/solution.py
+++ b/solution.py
@@ -13,7 +13,14 @@
     capacity = max(2, 3 * tile_rows // group_size)
     inner_pos = lax.axis_index("inner")
     outer_pos = lax.axis_index("outer")
-    piece = lax.all_gather(expander, "inner", axis=0, tiled=True)
+    ring = [expander]
+    for hop in range(15):
+        ring.append(lax.ppermute(ring[-1], "inner", [(dev, (dev + 1) % 16) for dev in range(16)]))
+    piece = jnp.roll(
+        jnp.concatenate(ring[::-1], axis=0),
+        (lax.axis_index("inner") + 1) * ring[0].shape[0],
+        axis=0,
+    )
     first_acc = jnp.dot(first_rows, piece, preferred_element_type=jnp.float32)
     second_acc = jnp.dot(second_rows, piece, preferred_element_type=jnp.float32)
     first_embed = first_acc.astype(jnp.bfloat16)

time: 296 us -> 381 us (1.29)
  waiting for transfers between devices: 107 us -> 174 us
  local copies, waits for them, and re-layouts: 83.5 us -> 101 us
    ppermute x0 -> x15, waiting for transfers between devices: none -> 158 us  [shards(): lax.ppermute(ring[-1], 'inner', [(dev, (dev + 1) % 16) for dev in range(1...]
    all_gather x1 -> x0, waiting for transfers between devices: 79.6 us -> none  [shards(): piece = lax.all_gather(expander, 'inner', axis=0, tiled=True)]
    unnamed x8 -> x63, local copies, waits for them, and re-layouts: 0.67 us -> 16.9 us
    all_to_all x1, waiting for transfers between devices: 26 us -> 14.9 us  [shards(): lax.all_to_all(send_rows, 'inner', split_axis=0, concat_axis=0, tiled=True)]
  transfers between devices with their start and end apart: 6 -> 20, of which waited for: 2 -> 16; matrix products, arithmetic and copies ran while one was open for 35% -> 28% of each run, Pallas kernels for 0% -> 0%
where the time goes in v1:
time: 381 us; the launch traced here: 378 us
  waiting for transfers between devices  174 us (46%)
  local copies, waits for them, and re-layouts  101 us (27%)
  blocking collectives  40.7 us (11%)
  starting transfers between devices  19.8 us (5%)
  other arithmetic  18.6 us (5%)
  between operations  15.2 us (4%)
  matrix products  8.77 us (2%)
    ppermute x15, waiting for transfers between devices, shards(): lax.ppermute(ring[-1], 'inner', [(dev, (dev + 1) % 16) for dev in range(1...  158 us
    psum x1, blocking collectives, shards(): lax.psum(jnp.sum(masked.astype(jnp.float32), axis=0), ('inner', 'outer'))  40.7 us
    scatter x1, local copies, waits for them, and re-layouts, shards(): send_rows = jnp.zeros((group_size, capacity, expand_width), jnp.bfloat16)...  36.8 us
    scatter x1, local copies, waits for them, and re-layouts, shards(): jnp.zeros((group_size, capacity), jnp.int32).at[target_dev, slot_pos]  36.1 us
    unnamed x63, local copies, waits for them, and re-layouts  16.9 us
    all_to_all x1, waiting for transfers between devices, shards(): lax.all_to_all(send_rows, 'inner', split_axis=0, concat_axis=0, tiled=True)  14.9 us
    gather x3, other arithmetic, shards(): dest_count = counts[target_dev]  10.2 us
  transfers between devices with their start and end apart: 20, of which 16 were waited for; matrix products, arithmetic and copies ran while one was open for 28% of the time, Pallas kernels for 0%

profile of v1, /device:TPU:0, one launch (start us, length us, event | category | flops | bytes accessed | tf_op | source)
XLA Modules:
  0.0 378.2 jit_solution(13407570571552110974)
XLA Ops:
  7.2 3.0 collective-permute-start
  10.2 10.5 %collective-permute-done = bf16[128,1024]{1,0:T(8,128)(2,1)S(1)} collective-permute-done((bf16[128,1024]{1,0:T(8,128)(2,1)}, bf16[128,1024]{1,0:T(8,128)(2,1)S(1)}, u32[]{:S(2)}, u32[]{:S(2)}) %collective-permute-start) | collective-permute-done | bytes 262176 | tf_op jit(solution)/shard_map/ppermute | solution.py:18
  20.7 11.1 %collective-permute-done.1 = bf16[128,1024]{1,0:T(8,128)(2,1)S(1)} collective-permute-done((bf16[128,1024]{1,0:T(8,128)(2,1)S(1)}, bf16[128,1024]{1,0:T(8,128)(2,1)S(1)}, u32[]{:S(2)}, u32[]{:S(2)}) %collective-permute-start.1) | collective-permute-done | bytes 262176 | tf_op jit(solution)/shard_map/ppermute | solution.py:18
  31.8 10.2 %collective-permute-done.2 = bf16[128,1024]{1,0:T(8,128)(2,1)S(1)} collective-permute-done((bf16[128,1024]{1,0:T(8,128)(2,1)S(1)}, bf16[128,1024]{1,0:T(8,128)(2,1)S(1)}, u32[]{:S(2)}, u32[]{:S(2)}) %collective-permute-start.2) | collective-permute-done | bytes 262176 | tf_op jit(solution)/shard_map/ppermute | solution.py:18
  42.0 10.0 %collective-permute-done.3 = bf16[128,1024]{1,0:T(8,128)(2,1)S(1)} collective-permute-done((bf16[128,1024]{1,0:T(8,128)(2,1)S(1)}, bf16[128,1024]{1,0:T(8,128)(2,1)S(1)}, u32[]{:S(2)}, u32[]{:S(2)}) %collective-permute-start.3) | collective-permute-done | bytes 262176 | tf_op jit(solution)/shard_map/ppermute | solution.py:18
  52.0 10.0 %collective-permute-done.4 = bf16[128,1024]{1,0:T(8,128)(2,1)S(1)} collective-permute-done((bf16[128,1024]{1,0:T(8,128)(2,1)S(1)}, bf16[128,1024]{1,0:T(8,128)(2,1)S(1)}, u32[]{:S(2)}, u32[]{:S(2)}) %collective-permute-start.4) | collective-permute-done | bytes 262176 | tf_op jit(solution)/shard_map/ppermute | solution.py:18
  61.9 10.0 %collective-permute-done.5 = bf16[128,1024]{1,0:T(8,128)(2,1)S(1)} collective-permute-done((bf16[128,1024]{1,0:T(8,128)(2,1)S(1)}, bf16[128,1024]{1,0:T(8,128)(2,1)S(1)}, u32[]{:S(2)}, u32[]{:S(2)}) %collective-permute-start.5) | collective-permute-done | bytes 262176 | tf_op jit(solution)/shard_map/ppermute | solution.py:18
  71.9 10.9 %collective-permute-done.6 = bf16[128,1024]{1,0:T(8,128)(2,1)S(1)} collective-permute-done((bf16[128,1024]{1,0:T(8,128)(2,1)S(1)}, bf16[128,1024]{1,0:T(8,128)(2,1)S(1)}, u32[]{:S(2)}, u32[]{:S(2)}) %collective-permute-start.6) | collective-permute-done | bytes 262176 | tf_op jit(solution)/shard_map/ppermute | solution.py:18
  82.8 12.0 %collective-permute-done.7 = bf16[128,1024]{1,0:T(8,128)(2,1)S(1)} collective-permute-done((bf16[128,1024]{1,0:T(8,128)(2,1)S(1)}, bf16[128,1024]{1,0:T(8,128)(2,1)S(1)}, u32[]{:S(2)}, u32[]{:S(2)}) %collective-permute-start.7) | collective-permute-done | bytes 262176 | tf_op jit(solution)/shard_map/ppermute | solution.py:18
  94.8 12.5 %collective-permute-done.8 = bf16[128,1024]{1,0:T(8,128)(2,1)S(1)} collective-permute-done((bf16[128,1024]{1,0:T(8,128)(2,1)S(1)}, bf16[128,1024]{1,0:T(8,128)(2,1)S(1)}, u32[]{:S(2)}, u32[]{:S(2)}) %collective-permute-start.8) | collective-permute-done | bytes 262176 | tf_op jit(solution)/shard_map/ppermute | solution.py:18
  108.0 11.9 %collective-permute-done.9 = bf16[128,1024]{1,0:T(8,128)(2,1)S(1)} collective-permute-done((bf16[128,1024]{1,0:T(8,128)(2,1)S(1)}, bf16[128,1024]{1,0:T(8,128)(2,1)S(1)}, u32[]{:S(2)}, u32[]{:S(2)}) %collective-permute-start.9) | collective-permute-done | bytes 262176 | tf_op jit(solution)/shard_map/ppermute | solution.py:18
  120.7 11.1 %collective-permute-done.10 = bf16[128,1024]{1,0:T(8,128)(2,1)S(1)} collective-permute-done((bf16[128,1024]{1,0:T(8,128)(2,1)S(1)}, bf16[128,1024]{1,0:T(8,128)(2,1)S(1)}, u32[]{:S(2)}, u32[]{:S(2)}) %collective-permute-start.10) | collective-permute-done | bytes 262176 | tf_op jit(solution)/shard_map/ppermute | solution.py:18
  132.5 10.2 %collective-permute-done.11 = bf16[128,1024]{1,0:T(8,128)(2,1)S(1)} collective-permute-done((bf16[128,1024]{1,0:T(8,128)(2,1)S(1)}, bf16[128,1024]{1,0:T(8,128)(2,1)S(1)}, u32[]{:S(2)}, u32[]{:S(2)}) %collective-permute-start.11) | collective-permute-done | bytes 262176 | tf_op jit(solution)/shard_map/ppermute | solution.py:18
  143.3 10.0 %collective-permute-done.12 = bf16[128,1024]{1,0:T(8,128)(2,1)S(1)} collective-permute-done((bf16[128,1024]{1,0:T(8,128)(2,1)S(1)}, bf16[128,1024]{1,0:T(8,128)(2,1)S(1)}, u32[]{:S(2)}, u32[]{:S(2)}) %collective-permute-start.12) | collective-permute-done | bytes 262176 | tf_op jit(solution)/shard_map/ppermute | solution.py:18
  154.0 10.1 %collective-permute-done.13 = bf16[128,1024]{1,0:T(8,128)(2,1)} collective-permute-done((bf16[128,1024]{1,0:T(8,128)(2,1)S(1)}, bf16[128,1024]{1,0:T(8,128)(2,1)}, u32[]{:S(2)}, u32[]{:S(2)}) %collective-permute-start.13) | collective-permute-done | bytes 262176 | tf_op jit(solution)/shard_map/ppermute | solution.py:18
  166.3 8.1 %collective-permute-done.14 = bf16[128,1024]{1,0:T(8,128)(2,1)} collective-permute-done((bf16[128,1024]{1,0:T(8,128)(2,1)}, bf16[128,1024]{1,0:T(8,128)(2,1)}, u32[]{:S(2)}, u32[]{:S(2)}) %collective-permute-start.14) | collective-permute-done | bytes 262176 | tf_op jit(solution)/shard_map/ppermute | solution.py:18
  184.8 3.2 copy-done.13
  189.3 2.8 fusion.20
  193.8 4.5 %compare_select_fusion.4 = (s32[256,1]{0,1:T(1,128)S(1)}, s32[256,1]{0,1:T(1,128)S(1)}) fusion(s32[]{:T(128)} %bitcast.13, s32[]{:T(128)} %bitcast.14, s32[]{:T(128)} %bitcast.15, s32[]{:T(128)} %bitcast.16, s32[]{:T(128)} %bitcast.17, s32[]{:T(128)} %bitcast.19, s32[]{:T(128)} %bitcast.18, s32[1,256,1]{1,2,0:T(1,128)S(1)} %copy-done.12), kind=kLoop, calls=%fused_computation.76 | loop fusion | flops 3840 | bytes 3100 | tf_op jit(solution)/shard_map/gather | solution.py:54
  198.9 36.1 %scatter_fusion = s32[16,48]{1,0:T(8,128)} fusion(s32[16,48]{1,0:T(8,128)} %broadcast.106, s32[256]{0:T(256)S(1)} %bitcast.67, s32[256]{0:T(256)S(1)} %bitcast.75), kind=kCustom, calls=%fused_computation.2 | custom fusion | bytes 5120 | tf_op jit(solution)/shard_map/scatter | solution.py:44
  235.1 3.5 all-to-all-start
  239.9 36.8 %scatter_fusion.1 = bf16[16,48,1024]{2,1,0:T(8,128)(2,1)} fusion(bf16[16,48,1024]{2,1,0:T(8,128)(2,1)} %broadcast_in_dim.22, s32[256]{0:T(256)S(1)} %bitcast.68, bf16[256,1024]{1,0:T(8,128)(2,1)S(1)} %get-tuple-element.32), kind=kCustom, calls=%fused_computation.3 | custom fusion | bytes 1574912 | tf_op jit(solution)/shard_map/scatter | solution.py:41
  276.8 6.9 %all-to-all-start.1 = ((bf16[16,48,1024]{2,1,0:T(8,128)(2,1)}), bf16[16,48,1024]{2,1,0:T(8,128)(2,1)S(1)}, u32[]{:S(2)}, u32[]{:S(2)}) async-start(bf16[16,48,1024]{2,1,0:T(8,128)(2,1)} %scatter_fusion.1), calls=%async_computation.2 | async-start | bytes 3145728 | tf_op jit(solution)/shard_map/all_to_all | solution.py:47
  283.8 4.6 %fusion.12 = bf16[256,1024]{0,1:T(8,128)(2,1)} fusion(bf16[4096,1024]{1,0:T(8,128)(2,1)} %copy-done.13, s32[]{:T(128)S(6)} %select_n.82, bf16[1,256,2048]{2,1,0:T(8,128)(2,1)} %param.7), kind=kOutput, calls=%fused_computation.13 | convolution fusion | flops 1074003968 | bytes 5767172 | tf_op jit(solution)/shard_map/dot_general | solution.py:25
  289.7 3.6 gather_fusion
  293.3 14.9 %all-to-all-done.1 = bf16[16,48,1024]{2,1,0:T(8,128)(2,1)S(1)} async-done(((bf16[16,48,1024]{2,1,0:T(8,128)(2,1)}), bf16[16,48,1024]{2,1,0:T(8,128)(2,1)S(1)}, u32[]{:S(2)}, u32[]{:S(2)}) %all-to-all-start.1) | async-done | bytes 1572896 | tf_op jit(solution)/shard_map/all_to_all | solution.py:47
  308.3 2.0 fusion.5
  311.6 6.3 %all-to-all-start.2 = ((f32[16,1,48]{2,1,0:T(1,128)}), f32[16,1,48]{2,1,0:T(1,128)S(1)}, u32[]{:S(2)}, u32[]{:S(2)}) async-start(f32[16,1,48]{2,1,0:T(1,128)} %compare_select_fusion), calls=%async_computation.3 | async-start | bytes 16384 | tf_op jit(solution)/shard_map/all_to_all | solution.py:53
  318.6 5.7 %select_select_fusion = s32[256]{0:T(256)S(1)} fusion(pred[256]{0:T(512)(128)(4,1)S(1)} %get-tuple-element.10, pred[256]{0:T(512)(128)(4,1)S(1)} %get-tuple-element.9, pred[256]{0:T(512)(128)(4,1)S(1)} %get-tuple-element.8, pred[256]{0:T(512)(128)(4,1)S(1)} %get-tuple-element.7, pred[256]{0:T(512)(128)(4,1)S(1)} %get-tuple-element.6, ...), kind=kLoop, calls=%fused_computation.87 | loop fusion | flops 2304 | bytes 4388 | tf_op jit(solution)/shard_map/gather | solution.py:54
  325.6 40.7 %psum.15 = f32[1024]{0:T(1024)S(1)} all-reduce(f32[1024]{0:T(1024)S(1)} %get-tuple-element.31), channel_id=1, replica_groups=mesh['inner'=16,'outer'=2] {'inner','outer'}, use_global_device_ids=true, to_apply=%region_3.4 | all-reduce | flops 1024 | bytes 8192 | tf_op jit(solution)/shard_map/psum | solution.py:58
  366.4 1.9 gather_fusion.1
  369.6 1.8 subtract_divide_fusion
  (109 shorter events, 26.2 us)
Async XLA Ops:
  7.2 180.8 %copy-start = (bf16[1,256,2048]{2,1,0:T(8,128)(2,1)S(1)}, bf16[1,256,2048]{2,1,0:T(8,128)(2,1)}, u32[]{:S(2)}) copy-start(bf16[1,256,2048]{2,1,0:T(8,128)(2,1)} %param.6) | copy-start | bytes 3145732
  7.2 177.5 %copy-start.1 = (bf16[128,1024]{1,0:T(8,128)(2,1)S(1)}, bf16[128,1024]{1,0:T(8,128)(2,1)}, u32[]{:S(2)}) copy-start(bf16[128,1024]{1,0:T(8,128)(2,1)} %param.8) | copy-start | bytes 786436
  7.2 310.8 %reduce-scatter.2.cloned.1.call-start = ((), (), s32[]{:S(2)}) async-start(), calls=%async_computation.4 | async-start | bytes 4456448 | tf_op jit(solution)/shard_map/reduce_scatter | solution.py:61
  7.2 13.5 %collective-permute-start = (bf16[128,1024]{1,0:T(8,128)(2,1)}, bf16[128,1024]{1,0:T(8,128)(2,1)S(1)}, u32[]{:S(2)}, u32[]{:S(2)}) collective-permute-start(bf16[128,1024]{1,0:T(8,128)(2,1)} %param.8), channel_id=1, source_target_pairs={{0,2},{2,4},{4,6},{6,8},{8,10},{10,12},{12,14},{14,16},{16,18},{18... | collective-permute-start | bytes 786440 | tf_op jit(solution)/shard_map/ppermute | solution.py:18
  20.7 11.1 %collective-permute-start.1 = (bf16[128,1024]{1,0:T(8,128)(2,1)S(1)}, bf16[128,1024]{1,0:T(8,128)(2,1)S(1)}, u32[]{:S(2)}, u32[]{:S(2)}) collective-permute-start(bf16[128,1024]{1,0:T(8,128)(2,1)S(1)} %collective-permute-done), channel_id=1, source_target_pairs={{0,2},{2,4},{4,6},{6,8},{8,10},{10,12},{12,14},{14,16},{16,18},{18... | collective-permute-start | bytes 786440 | tf_op jit(solution)/shard_map/ppermute | solution.py:18
  31.8 10.2 %collective-permute-start.2 = (bf16[128,1024]{1,0:T(8,128)(2,1)S(1)}, bf16[128,1024]{1,0:T(8,128)(2,1)S(1)}, u32[]{:S(2)}, u32[]{:S(2)}) collective-permute-start(bf16[128,1024]{1,0:T(8,128)(2,1)S(1)} %collective-permute-done.1), channel_id=1, source_target_pairs={{0,2},{2,4},{4,6},{6,8},{8,10},{10,12},{12,14},{14,16},{16,18},{18... | collective-permute-start | bytes 786440 | tf_op jit(solution)/shard_map/ppermute | solution.py:18
  42.0 10.0 %collective-permute-start.3 = (bf16[128,1024]{1,0:T(8,128)(2,1)S(1)}, bf16[128,1024]{1,0:T(8,128)(2,1)S(1)}, u32[]{:S(2)}, u32[]{:S(2)}) collective-permute-start(bf16[128,1024]{1,0:T(8,128)(2,1)S(1)} %collective-permute-done.2), channel_id=1, source_target_pairs={{0,2},{2,4},{4,6},{6,8},{8,10},{10,12},{12,14},{14,16},{16,18},{18... | collective-permute-start | bytes 786440 | tf_op jit(solution)/shard_map/ppermute | solution.py:18
  52.0 10.0 %collective-permute-start.4 = (bf16[128,1024]{1,0:T(8,128)(2,1)S(1)}, bf16[128,1024]{1,0:T(8,128)(2,1)S(1)}, u32[]{:S(2)}, u32[]{:S(2)}) collective-permute-start(bf16[128,1024]{1,0:T(8,128)(2,1)S(1)} %collective-permute-done.3), channel_id=1, source_target_pairs={{0,2},{2,4},{4,6},{6,8},{8,10},{10,12},{12,14},{14,16},{16,18},{18... | collective-permute-start | bytes 786440 | tf_op jit(solution)/shard_map/ppermute | solution.py:18
  61.9 10.0 %collective-permute-start.5 = (bf16[128,1024]{1,0:T(8,128)(2,1)S(1)}, bf16[128,1024]{1,0:T(8,128)(2,1)S(1)}, u32[]{:S(2)}, u32[]{:S(2)}) collective-permute-start(bf16[128,1024]{1,0:T(8,128)(2,1)S(1)} %collective-permute-done.4), channel_id=1, source_target_pairs={{0,2},{2,4},{4,6},{6,8},{8,10},{10,12},{12,14},{14,16},{16,18},{18... | collective-permute-start | bytes 786440 | tf_op jit(solution)/shard_map/ppermute | solution.py:18
  71.9 10.9 %collective-permute-start.6 = (bf16[128,1024]{1,0:T(8,128)(2,1)S(1)}, bf16[128,1024]{1,0:T(8,128)(2,1)S(1)}, u32[]{:S(2)}, u32[]{:S(2)}) collective-permute-start(bf16[128,1024]{1,0:T(8,128)(2,1)S(1)} %collective-permute-done.5), channel_id=1, source_target_pairs={{0,2},{2,4},{4,6},{6,8},{8,10},{10,12},{12,14},{14,16},{16,18},{18... | collective-permute-start | bytes 786440 | tf_op jit(solution)/shard_map/ppermute | solution.py:18
  82.8 12.1 %collective-permute-start.7 = (bf16[128,1024]{1,0:T(8,128)(2,1)S(1)}, bf16[128,1024]{1,0:T(8,128)(2,1)S(1)}, u32[]{:S(2)}, u32[]{:S(2)}) collective-permute-start(bf16[128,1024]{1,0:T(8,128)(2,1)S(1)} %collective-permute-done.6), channel_id=1, source_target_pairs={{0,2},{2,4},{4,6},{6,8},{8,10},{10,12},{12,14},{14,16},{16,18},{18... | collective-permute-start | bytes 786440 | tf_op jit(solution)/shard_map/ppermute | solution.py:18
  94.8 12.5 %collective-permute-start.8 = (bf16[128,1024]{1,0:T(8,128)(2,1)S(1)}, bf16[128,1024]{1,0:T(8,128)(2,1)S(1)}, u32[]{:S(2)}, u32[]{:S(2)}) collective-permute-start(bf16[128,1024]{1,0:T(8,128)(2,1)S(1)} %collective-permute-done.7), channel_id=1, source_target_pairs={{0,2},{2,4},{4,6},{6,8},{8,10},{10,12},{12,14},{14,16},{16,18},{18... | collective-permute-start | bytes 786440 | tf_op jit(solution)/shard_map/ppermute | solution.py:18
  108.0 11.9 %collective-permute-start.9 = (bf16[128,1024]{1,0:T(8,128)(2,1)S(1)}, bf16[128,1024]{1,0:T(8,128)(2,1)S(1)}, u32[]{:S(2)}, u32[]{:S(2)}) collective-permute-start(bf16[128,1024]{1,0:T(8,128)(2,1)S(1)} %collective-permute-done.8), channel_id=1, source_target_pairs={{0,2},{2,4},{4,6},{6,8},{8,10},{10,12},{12,14},{14,16},{16,18},{18... | collective-permute-start | bytes 786440 | tf_op jit(solution)/shard_map/ppermute | solution.py:18
  120.7 11.1 %collective-permute-start.10 = (bf16[128,1024]{1,0:T(8,128)(2,1)S(1)}, bf16[128,1024]{1,0:T(8,128)(2,1)S(1)}, u32[]{:S(2)}, u32[]{:S(2)}) collective-permute-start(bf16[128,1024]{1,0:T(8,128)(2,1)S(1)} %collective-permute-done.9), channel_id=1, source_target_pairs={{0,2},{2,4},{4,6},{6,8},{8,10},{10,12},{12,14},{14,16},{16,18},{18... | collective-permute-start | bytes 786440 | tf_op jit(solution)/shard_map/ppermute | solution.py:18
  132.5 10.2 %collective-permute-start.11 = (bf16[128,1024]{1,0:T(8,128)(2,1)S(1)}, bf16[128,1024]{1,0:T(8,128)(2,1)S(1)}, u32[]{:S(2)}, u32[]{:S(2)}) collective-permute-start(bf16[128,1024]{1,0:T(8,128)(2,1)S(1)} %collective-permute-done.10), channel_id=1, source_target_pairs={{0,2},{2,4},{4,6},{6,8},{8,10},{10,12},{12,14},{14,16},{16,18},{18... | collective-permute-start | bytes 786440 | tf_op jit(solution)/shard_map/ppermute | solution.py:18
  142.6 0.7 copy-start.8
  143.3 10.0 %collective-permute-start.12 = (bf16[128,1024]{1,0:T(8,128)(2,1)S(1)}, bf16[128,1024]{1,0:T(8,128)(2,1)S(1)}, u32[]{:S(2)}, u32[]{:S(2)}) collective-permute-start(bf16[128,1024]{1,0:T(8,128)(2,1)S(1)} %collective-permute-done.11), channel_id=1, source_target_pairs={{0,2},{2,4},{4,6},{6,8},{8,10},{10,12},{12,14},{14,16},{16,18},{18... | collective-permute-start | bytes 786440 | tf_op jit(solution)/shard_map/ppermute | solution.py:18
  154.0 10.1 %collective-permute-start.13 = (bf16[128,1024]{1,0:T(8,128)(2,1)S(1)}, bf16[128,1024]{1,0:T(8,128)(2,1)}, u32[]{:S(2)}, u32[]{:S(2)}) collective-permute-start(bf16[128,1024]{1,0:T(8,128)(2,1)S(1)} %collective-permute-done.12), channel_id=1, source_target_pairs={{0,2},{2,4},{4,6},{6,8},{8,10},{10,12},{12,14},{14,16},{16,18},{18... | collective-permute-start | bytes 786440 | tf_op jit(solution)/shard_map/ppermute | solution.py:18
  164.1 10.3 %collective-permute-start.14 = (bf16[128,1024]{1,0:T(8,128)(2,1)}, bf16[128,1024]{1,0:T(8,128)(2,1)}, u32[]{:S(2)}, u32[]{:S(2)}) collective-permute-start(bf16[128,1024]{1,0:T(8,128)(2,1)} %collective-permute-done.13), channel_id=1, source_target_pairs={{0,2},{2,4},{4,6},{6,8},{8,10},{10,12},{12,14},{14,16},{16,18},{18... | collective-permute-start | bytes 786440 | tf_op jit(solution)/shard_map/ppermute | solution.py:18
  164.1 20.2 %copy-start.11 = (bf16[128,1024]{1,0:T(8,128)(2,1)S(1)}, bf16[128,1024]{1,0:T(8,128)(2,1)}, u32[]{:S(2)}) copy-start(bf16[128,1024]{1,0:T(8,128)(2,1)} %copy-done.10) | copy-start | bytes 786436
  164.1 20.3 %copy-start.9 = (bf16[128,1024]{1,0:T(8,128)(2,1)S(1)}, bf16[128,1024]{1,0:T(8,128)(2,1)}, u32[]{:S(2)}) copy-start(bf16[128,1024]{1,0:T(8,128)(2,1)} %copy-done.8) | copy-start | bytes 786436
  164.1 20.3 %copy-start.7 = (bf16[128,1024]{1,0:T(8,128)(2,1)S(1)}, bf16[128,1024]{1,0:T(8,128)(2,1)}, u32[]{:S(2)}) copy-start(bf16[128,1024]{1,0:T(8,128)(2,1)} %copy-done.6) | copy-start | bytes 786436
  164.1 20.3 %copy-start.5 = (bf16[128,1024]{1,0:T(8,128)(2,1)S(1)}, bf16[128,1024]{1,0:T(8,128)(2,1)}, u32[]{:S(2)}) copy-start(bf16[128,1024]{1,0:T(8,128)(2,1)} %copy-done.4) | copy-start | bytes 786436
  164.1 20.4 %copy-start.3 = (bf16[128,1024]{1,0:T(8,128)(2,1)S(1)}, bf16[128,1024]{1,0:T(8,128)(2,1)}, u32[]{:S(2)}) copy-start(bf16[128,1024]{1,0:T(8,128)(2,1)} %copy-done.2) | copy-start | bytes 786436
  184.7 7.4 %copy-start.12 = (s32[1,256,1]{1,2,0:T(1,128)S(1)}, s32[1,256,1]{1,2,0:T(1,128)}, u32[]{:S(2)}) copy-start(s32[1,256,1]{1,2,0:T(1,128)} %param.10) | copy-start | bytes 3076
  184.7 8.3 %copy-start.15 = (s32[2,16]{1,0:T(2,128)S(1)}, s32[2,16]{1,0:T(2,128)}, u32[]{:S(2)}) copy-start(s32[2,16]{1,0:T(2,128)} %param.9) | copy-start | bytes 388
  184.8 3.2 copy-start.13
  188.0 10.9 %copy-start.14 = (s32[1,256]{1,0:T(1,128)S(1)}, s32[1,256]{1,0:T(1,128)}, u32[]{:S(2)}) copy-start(s32[1,256]{1,0:T(1,128)} %param.11) | copy-start | bytes 3076
  235.1 41.7 %all-to-all-start = ((s32[16,1,48]{2,1,0:T(1,128)}), s32[16,1,48]{2,1,0:T(1,128)S(1)}, u32[]{:S(2)}, u32[]{:S(2)}) async-start(s32[16,1,48]{2,1,0:T(1,128)} %bitcast.29), calls=%async_computation.1 | async-start | bytes 16384 | tf_op jit(solution)/shard_map/all_to_all | solution.py:48
  276.8 31.5 %all-to-all-start.1 = ((bf16[16,48,1024]{2,1,0:T(8,128)(2,1)}), bf16[16,48,1024]{2,1,0:T(8,128)(2,1)S(1)}, u32[]{:S(2)}, u32[]{:S(2)}) async-start(bf16[16,48,1024]{2,1,0:T(8,128)(2,1)} %scatter_fusion.1), calls=%async_computation.2 | async-start | bytes 3145728 | tf_op jit(solution)/shard_map/all_to_all | solution.py:47
  311.6 54.8 %all-to-all-start.2 = ((f32[16,1,48]{2,1,0:T(1,128)}), f32[16,1,48]{2,1,0:T(1,128)S(1)}, u32[]{:S(2)}, u32[]{:S(2)}) async-start(f32[16,1,48]{2,1,0:T(1,128)} %compare_select_fusion), calls=%async_computation.3 | async-start | bytes 16384 | tf_op jit(solution)/shard_map/all_to_all | solution.py:53
  317.9 51.7 %all-reduce.2.cloned.1.call-start = ((), (), s32[]{:S(2)}) async-start(), calls=%async_computation.5 | async-start | bytes 524288 | tf_op jit(solution)/shard_map/psum | solution.py:69
  (4 other events, 2.8 us)
Sparse Core Ops, SparseCore 0:
  192.3 99.0 reduce-scatter.1
  321.1 19.5 all-reduce.1
